TPU v7x, 768 devices: a whole 4x8x12 slice. The times are simulated.
768 devices in a mesh: fsdp: 64 (over y, x, core), tp: 12 (over z).
Axes of the slice: x: 4, y: 8, z: 12, core: 2. Of those that a mesh axis runs over, the one named last changes fastest.
Arguments:
- momentum: float32 [8192, 27648], P('fsdp', 'tp'), may hold values from -60 to 60
- gradient: bfloat16 [8192, 27648], P('fsdp', 'tp'), may hold values from -6 to 6
- right_factor: float32 [256, 27648], P('fsdp', 'tp'), may hold values from -6 to 6
Outputs:
- next_momentum: float32 [8192, 27648], P('fsdp', 'tp')
- update: bfloat16 [8192, 27648], P('fsdp', 'tp')
- next_factor: float32 [256, 27648], P('fsdp', 'tp')
All inputs are finite; a program needn't handle non-finite values.
Results may differ from a plain program's by a relative error of at most 0.001.
Values sent between devices are 32-bit elements; how exact they have to be, the bound alone decides.
A program may use at most 32 MiB of HBM per device.

v0:
```python
import math

import jax
import jax.numpy as jnp
from jax import lax
from jax.sharding import PartitionSpec as P

ROWS = 8192
COLS = 27648
RANK = 256


decay_rate = 0.9
norm_eps = 1e-08


def shards(momentum, gradient, right_factor):
    highest = lax.Precision.HIGHEST
    buffer = momentum + gradient.astype(jnp.float32)
    partial_left = lax.dot_general(
        buffer,
        lax.all_gather(right_factor, "fsdp", axis=0, tiled=True),
        (((1,), (1,)), ((), ())),
        precision=highest,
        preferred_element_type=jnp.float32,
    )
    left_factor = lax.psum(partial_left, "tp")
    gram_local = jnp.dot(left_factor.T, left_factor, precision=highest)
    gram_total = lax.psum(gram_local, "fsdp")
    lower_factor = jnp.linalg.cholesky(gram_total)
    left_basis = jax.scipy.linalg.solve_triangular(lower_factor, left_factor.T, lower=True).T
    share_rows = right_factor.shape[0]
    right_rows = lax.psum(jnp.dot(left_basis.T, buffer, precision=highest), "fsdp")
    squares = jnp.sum(right_rows * right_rows, axis=1)
    norm_total = lax.psum(squares, "tp")
    inverse_norm = 1.0 / (jnp.sqrt(norm_total) + norm_eps)
    whole_factor = right_rows * inverse_norm[:, None]
    first_row = lax.axis_index("fsdp") * share_rows
    next_factor = lax.dynamic_slice_in_dim(whole_factor, first_row, share_rows, 0)
    next_momentum = buffer - (1.0 - decay_rate) * jnp.dot(left_basis, right_rows, precision=highest)
    update_scale = math.sqrt(ROWS * COLS / RANK)
    update = (update_scale * jnp.dot(left_basis, whole_factor, precision=highest)).astype(
        jnp.bfloat16
    )
    return (next_momentum, update, next_factor)


def solution(mesh):
    return jax.shard_map(
        shards,
        mesh=mesh,
        in_specs=(P("fsdp", "tp"), P("fsdp", "tp"), P("fsdp", "tp")),
        out_specs=(P("fsdp", "tp"), P("fsdp", "tp"), P("fsdp", "tp")),
        check_vma=False,
    )
```

profile of v0, /device:TPU:1, one launch (start us, length us, event | category | flops | bytes accessed | tf_op | source)
XLA Modules:
  0.0 732.4 jit_solution(7262686648907971541)
XLA Ops:
  7.2 0.0 all-gather.3.cloned.1.call-start
  7.2 0.7 all-gather.3.cloned.1.call-update
  7.9 0.0 copy-start.1
  7.9 0.0 all-reduce.5.cloned.1.call-start
  8.0 100.1 %all-gather.3.cloned.1.call-done = f32[64,4,2304]{2,1,0:T(4,128)} async-done(((f32[1,4,2304]{2,1,0:T(4,128)}), f32[64,4,2304]{2,1,0:T(4,128)}) %all-gather.3.cloned.1.call-update) | async-done | bytes 2359312 | tf_op jit(solution)/shard_map/all_gather | solution.py:22
  108.1 2.6 reshape.46
  110.7 0.0 copy-done.1
  110.7 4.2 fusion.3
  114.9 0.0 all-reduce.5.cloned.1.call-update
  114.9 0.0 all-reduce.7.cloned.1.call-start
  115.0 101.2 %all-reduce.5.cloned.1.call-done = f32[128,256]{1,0:T(8,128)} async-done(((f32[128,256]{1,0:T(8,128)}), f32[128,256]{1,0:T(8,128)}) %all-reduce.5.cloned.1.call-update) | async-done | bytes 131088 | tf_op jit(solution)/shard_map/psum | solution.py:27
  216.2 2.1 fusion.16
  218.3 0.0 all-reduce.7.cloned.1.call-update
  218.3 0.2 all-reduce.9.cloned.1.call-start
  218.6 204.3 %all-reduce.7.cloned.1.call-done = f32[256,256]{0,1:T(8,128)} async-done(((f32[256,256]{0,1:T(8,128)}), f32[256,256]{0,1:T(8,128)}) %all-reduce.7.cloned.1.call-update) | async-done | bytes 262160 | tf_op jit(solution)/shard_map/psum | solution.py:29
  422.9 1.1 copy.9
  424.0 1.0 fusion.4
  425.0 11.7 %cholesky.50 = f32[128,128]{1,0:T(8,128)S(1)} custom-call(f32[128,128]{1,0:T(8,128)S(1)} %cholesky.118), custom_call_target="Cholesky" | custom-call | tf_op jit(solution)/shard_map/jit(cholesky)/cholesky | solution.py:30
  436.7 9.8 %custom-call.15 = f32[1,128,128]{1,2,0:T(8,128)S(1)} custom-call(f32[1,128,128]{2,1,0:T(8,128)S(1)} %get-tuple-element.24), custom_call_target="InvertDiagBlocksLowerTriangular" | custom-call | tf_op jit(solution)/shard_map/jit(cholesky)/cholesky | solution.py:30
  446.5 0.0 copy-start.6
  446.6 0.2 constant_dynamic-update-slice_fusion
  446.8 0.0 copy-start.2
  446.8 0.3 convolution_subtract_fusion.1
  447.1 11.7 %cholesky.105 = f32[128,128]{1,0:T(8,128)S(1)} custom-call(f32[128,128]{1,0:T(8,128)S(1)} %convolution_subtract_fusion.1), custom_call_target="Cholesky" | custom-call | tf_op jit(solution)/shard_map/jit(cholesky)/cholesky | solution.py:30
  458.8 0.6 compare_reduce_fusion
  460.8 0.1 triangular_solve.57
  460.9 4.2 while.1
  461.1 0.6 fusion.27
  461.6 1.4 bitcast_dynamic-update-slice_fusion.2
  463.1 0.6 fusion.27
  463.7 1.4 bitcast_dynamic-update-slice_fusion.2
  465.0 19.7 %custom-call.16 = f32[2,128,128]{1,2,0:T(8,128)S(1)} custom-call(f32[2,128,128]{2,1,0:T(8,128)S(1)} %get-tuple-element.10), custom_call_target="InvertDiagBlocksLowerTriangular" | custom-call | tf_op jit(solution)/shard_map/jit(_solve_triangular)/triangular_solve | solution.py:31
  484.7 0.0 copy-done.6
  484.7 0.3 fusion.7
  485.0 0.0 copy-start.4
  485.0 0.3 convolution_subtract_fusion
  485.3 0.3 fusion.6
  485.6 0.0 copy-done.4
  485.7 0.0 copy-start.7
  485.7 0.6 copy-done.7
  486.3 0.0 copy-done.2
  486.3 3.4 fusion.2
  489.7 0.0 all-reduce.9.cloned.1.call-update
  489.7 208.0 %all-reduce.9.cloned.1.call-done = f32[256,2304]{1,0:T(8,128)} async-done(((f32[256,2304]{1,0:T(8,128)}), f32[256,2304]{1,0:T(8,128)}) %all-reduce.9.cloned.1.call-update) | async-done | bytes 2359312 | tf_op jit(solution)/shard_map/psum | solution.py:33
  697.8 0.0 copy-start
  697.8 2.1 multiply_reduce_fusion
  699.8 19.9 %psum.31 = f32[256]{0:T(256)S(1)} all-reduce(f32[256]{0:T(256)S(1)} %multiply_reduce_fusion), channel_id=1, replica_groups=mesh['fsdp'=64,'tp'=12] {'tp'}, use_global_device_ids=true, to_apply=%region_8.9 | all-reduce | flops 256 | bytes 2048 | tf_op jit(solution)/shard_map/psum | solution.py:35
  719.7 0.0 copy-done
  719.7 0.0 copy-start.5
  719.7 0.0 copy-start.8
  719.7 0.2 broadcast_multiply_fusion
  719.9 0.6 copy-done.5
  720.5 0.0 copy-done.8
  720.6 0.0 copy-start.3
  720.6 2.2 fusion.1
  722.7 0.6 constant_dynamic-slice_fusion.1
  723.4 0.0 copy-done.3
  723.4 2.5 fusion
  (10 shorter events, 0.2 us)
Async XLA Ops:
  7.2 100.9 %all-gather.3.cloned.1.call-start = ((), (), s32[]{:S(2)}) async-start(), calls=%async_computation.3 | async-start | bytes 2396160 | tf_op jit(solution)/shard_map/all_gather | solution.py:22
  7.9 102.8 %copy-start.1 = (f32[128,2304]{1,0:T(8,128)S(1)}, f32[128,2304]{1,0:T(8,128)}, u32[]{:S(2)}) copy-start(f32[128,2304]{1,0:T(8,128)} %param.3) | copy-start | bytes 3538948
  7.9 208.3 %all-reduce.5.cloned.1.call-start = ((), (), s32[]{:S(2)}) async-start(), calls=%async_computation | async-start | bytes 262144 | tf_op jit(solution)/shard_map/psum | solution.py:27
  114.9 308.0 %all-reduce.7.cloned.1.call-start = ((), (), s32[]{:S(2)}) async-start(), calls=%async_computation.1 | async-start | bytes 524288 | tf_op jit(solution)/shard_map/psum | solution.py:29
  218.3 479.4 %all-reduce.9.cloned.1.call-start = ((), (), s32[]{:S(2)}) async-start(), calls=%async_computation.2 | async-start | bytes 4718592 | tf_op jit(solution)/shard_map/psum | solution.py:33
  446.5 38.2 %copy-start.6 = (f32[128,256]{1,0:T(8,128)S(1)}, f32[128,256]{1,0:T(8,128)}, u32[]{:S(2)}) copy-start(f32[128,256]{1,0:T(8,128)} %all-reduce.5.cloned.1.call-done) | copy-start | bytes 393220
  446.8 39.5 %copy-start.2 = (bf16[128,2304]{1,0:T(8,128)(2,1)S(1)}, bf16[128,2304]{1,0:T(8,128)(2,1)}, u32[]{:S(2)}) copy-start(bf16[128,2304]{1,0:T(8,128)(2,1)} %param.4) | copy-start | bytes 1769476
  485.0 0.6 copy-start.4
  485.7 0.6 copy-start.7
  697.8 21.9 %copy-start = (f32[256,2304]{1,0:T(8,128)S(1)}, f32[256,2304]{1,0:T(8,128)}, u32[]{:S(2)}) copy-start(f32[256,2304]{1,0:T(8,128)} %all-reduce.9.cloned.1.call-done) | copy-start | bytes 7077892
  719.7 0.8 copy-start.5
  719.7 0.9 copy-start.8
  720.6 2.8 copy-start.3
Sparse Core Ops, SparseCore 0:
  11.8 96.1 all-gather.2
  115.0 101.1 all-reduce.4
  220.7 202.1 all-reduce.6
  489.9 207.8 all-reduce.8
where the time goes:
time: 739 us; the launch traced here: 732 us
  waiting for transfers between devices  614 us (83%)
  other arithmetic  56.9 us (8%)
  blocking collectives  19.9 us (3%)
  matrix products  15.6 us (2%)
  between operations  15.3 us (2%)
  local copies, waits for them, and re-layouts  9.7 us (1%)
    psum x1, waiting for transfers between devices, shards(): lax.psum(jnp.dot(left_basis.T, buffer, precision=highest), 'fsdp')  208 us
    psum x1, waiting for transfers between devices, shards(): gram_total = lax.psum(gram_local, 'fsdp')  204 us
    psum x1, waiting for transfers between devices, shards(): left_factor = lax.psum(partial_left, 'tp')  101 us
    all_gather x1, waiting for transfers between devices, shards(): lax.all_gather(right_factor, 'fsdp', axis=0, tiled=True)  100 us
    another operation x6, other arithmetic, shards(): lower_factor = jnp.linalg.cholesky(gram_total)  34 us
    psum x1, blocking collectives, shards(): norm_total = lax.psum(squares, 'tp')  19.9 us
    another operation x3, other arithmetic, shards(): jax.scipy.linalg.solve_triangular(lower_factor, left_factor.T, lower=True)  19.7 us
  transfers between devices with their start and end apart: 4, of which 4 were waited for; matrix products, arithmetic and copies ran while one was open for 0% of the time, Pallas kernels for 0%

commit v1 on v0

v1 whole, which is shorter than its diff:
```python
import itertools
import math

import jax
import jax.numpy as jnp
from jax import lax
from jax.experimental import pallas as pl
from jax.experimental.pallas import tpu as pltpu
from jax.sharding import PartitionSpec as P

ROWS = 8192
COLS = 27648
RANK = 256

decay_rate = 0.9
norm_eps = 1e-08

MESH = pl.DeviceIdType.MESH
HIGHEST = lax.Precision.HIGHEST
f32 = jnp.float32
bf16 = jnp.bfloat16

NX, NY, NZ = 4, 8, 12
LOCAL_ROWS = ROWS // 64
LOCAL = COLS // NZ
HALF = LOCAL // 2
CUT = 256
REST = HALF - CUT
CHUNK = 384
BLOCK = 16
OUTWARD = (1, 7, 2, 6, 3, 5, 4)
INWARD = (4, 3, 5, 2, 6, 1, 7)
COPIES = 384
VMEM_LIMIT = 48 << 20


def dot(a, b, dims, precision=HIGHEST):
    return lax.dot_general(a, b, (dims, ((), ())), precision=precision, preferred_element_type=f32)


def split3(a):
    first = a.astype(bf16)
    rest = a - first.astype(f32)
    second = rest.astype(bf16)
    third = (rest - second.astype(f32)).astype(bf16)
    return first, second, third


def factor_step(work, k):
    b, n = BLOCK, RANK
    first = pl.multiple_of(k * b, b)
    rows = work[pl.ds(first, b), :]
    lane = lax.broadcasted_iota(jnp.int32, (b, n), 1)
    row = lax.broadcasted_iota(jnp.int32, (b, n), 0)
    row128 = lax.broadcasted_iota(jnp.int32, (b, 128), 0)
    here = jnp.where(first >= 128, rows[:, 128:], rows[:, :128])
    here = pltpu.roll(here, lax.rem(128 - lax.rem(first, 128), 128), 1)
    column = [jnp.broadcast_to(here[:, j : j + 1], (b, 128)) for j in range(b)]
    inside = (lane >= first) & (lane < first + b)
    rows = jnp.where(inside, jnp.where(lane - first == row, 1.0, 0.0), rows)
    low, high = rows[:, :128], rows[:, 128:]
    pivots = jnp.ones((b, 128), f32)
    for j in range(b):
        pivot = column[j][j : j + 1, :]
        scaled = jnp.where(row128 > j, column[j] * (1.0 / pivot), 0.0)
        pivots = jnp.where(row128 == j, pivot, pivots)
        for i in range(j + 1, b):
            column[i] = column[i] - scaled * column[i][j : j + 1, :]
        low = low - scaled * low[j : j + 1, :]
        high = high - scaled * high[j : j + 1, :]
    scale = lax.rsqrt(pivots)
    rows = jnp.concatenate([low * scale, high * scale], axis=1)
    ahead = jnp.where(lane >= first + b, rows, 0.0)
    a1, a2, a3 = split3(ahead)
    r1, r2, r3 = split3(rows)
    change = dot(
        jnp.concatenate([a1, a1, a2, a2, a1, a3], axis=0),
        jnp.concatenate([r1, r2, r1, r2, r3, r1], axis=0),
        ((0,), (0,)),
        None,
    )
    lanes = lax.broadcasted_iota(jnp.int32, (n, n), 1)
    work[...] = jnp.where((lanes >= first) & (lanes < first + b), 0.0, work[...]) - change
    work[pl.ds(first, b), :] = rows


def kernel(
    mom, grad, rf, nm, up, nf,
    buf, rg, sib4, lp, zr, lf, gp, gs, gr, gsum, gr2, gg, mp, ms, ra, sa, ra2, rb, sb, rb2, mg, work, rr, sq, sqr,
    send, recv,
):
    f, z = lax.axis_index("fsdp"), lax.axis_index("tp")
    c, x, y = lax.rem(f, 2), lax.rem(lax.div(f, 2), NX), lax.div(f, 2 * NX)

    def wrap(v, n):
        return lax.rem(v + n, n)

    def at(dx=0, dy=0, dz=0, core=None):
        chip = wrap(y + dy, NY) * NX + wrap(x + dx, NX)
        return (chip * 2 + (c if core is None else core), wrap(z + dz, NZ))

    sibling = at(core=1 - c)
    number = itertools.count()
    started = []

    def go(src, dst, to):
        i = next(number)
        copy = pltpu.make_async_remote_copy(
            src_ref=src, dst_ref=dst, send_sem=send.at[i], recv_sem=recv.at[i], device_id=to, device_id_type=MESH
        )
        copy.start()
        started.append(copy)
        return copy

    peers = [sibling] + [at(dx=e) for e in range(1, NX)] + [at(dy=e) for e in range(1, NY)]
    peers += [at(dz=e) for e in range(1, NZ)]
    barrier = pltpu.get_barrier_semaphore()
    for peer in peers:
        pl.semaphore_signal(barrier, inc=1, device_id=peer, device_id_type=MESH)
    buf[...] = mom[...] + grad[...].astype(f32)
    pl.semaphore_wait(barrier, len(peers))

    class Gather:
        def __init__(self, ref):
            self.half = ref.at[c]
            self.cols_a, self.cols_b = pl.ds(0, CUT), pl.ds(CUT, REST)

        def start(self):
            half, a, b = self.half, self.cols_a, self.cols_b
            own_a, own_b = half.at[y, x, :, a], half.at[y, x, :, b]
            self.ax = [go(own_a, own_a, at(dx=e)) for e in range(1, NX)]
            self.by = {e: go(own_b, own_b, at(dy=e)) for e in OUTWARD}
            self.bx = {0: [go(own_b, own_b, at(dx=g)) for g in range(1, NX)]}

        def pass_a(self):
            for copy in self.ax:
                copy.wait_recv()
            line = self.half.at[y, :, :, self.cols_a]
            self.ay = [go(line, line, at(dy=e)) for e in INWARD]

        def pass_b(self, e):
            self.by[e].wait_recv()
            block = self.half.at[wrap(y - e, NY), x, :, self.cols_b]
            self.bx[e] = [go(block, block, at(dx=g)) for g in range(1, NX)]

        def hand_b(self, e):
            for copy in self.bx[e]:
                copy.wait_recv()
            line = self.half.at[wrap(y - e, NY), :, :, self.cols_b]
            self.given = getattr(self, "given", []) + [go(line, line, sibling)]

        def hand_a(self):
            for copy in self.ay:
                copy.wait_recv()
            part = self.half.at[:, :, :, self.cols_a]
            self.given.append(go(part, part, sibling))

        def finish(self):
            for copy in self.given:
                copy.wait_recv()

    other_cols = pl.ds(pl.multiple_of((1 - c) * HALF, 128), HALF)
    swap = go(rf.at[:, other_cols], sib4, sibling)
    swap.wait_recv()
    mine, theirs = rf[:, pl.ds(pl.multiple_of(c * HALF, 128), HALF)], sib4[...]
    rg[c, y, x, 0:4, :] = jnp.where(c == 0, mine, theirs)
    rg[c, y, x, 4:8, :] = jnp.where(c == 0, theirs, mine)
    gather = Gather(rg)
    gather.start()
    gather.pass_b(1)
    gather.pass_b(7)
    gather.pass_a()
    for e in OUTWARD[2:]:
        gather.pass_b(e)
    for e in (0,) + OUTWARD:
        gather.hand_b(e)
    gather.hand_a()

    def partial_left(core, total):
        def body(i, total):
            k = pl.multiple_of(i * CHUNK, 128)
            right = rg[core, :, :, :, pl.ds(k, CHUNK)].reshape(RANK, CHUNK)
            left = buf[:, pl.ds(pl.multiple_of(core * HALF + k, 128), CHUNK)]
            return total + dot(right, left, ((1,), (1,)))

        return lax.fori_loop(0, HALF // CHUNK, body, total)

    total = partial_left(c, jnp.zeros((RANK, LOCAL_ROWS), f32))
    gather.finish()
    total = partial_left(1 - c, total)

    lp[0:32] = total.reshape(32, 8, LOCAL_ROWS)
    lp[32:36] = jnp.zeros((4, 8, LOCAL_ROWS), f32)
    own_tiles = pl.ds(z * 3, 3)
    parts = []
    for e in range(1, NZ):
        parts.append(go(lp.at[pl.ds(wrap(z + e, NZ) * 3, 3)], zr.at[e - 1], at(dz=e)))
    for copy in parts:
        copy.wait_recv()
    tiles = lp[own_tiles]
    for e in range(1, NZ):
        tiles = tiles + zr[e - 1]
    lf[own_tiles] = tiles
    parts = [go(lf.at[own_tiles], lf.at[own_tiles], at(dz=e)) for e in range(1, NZ)]
    for copy in parts:
        copy.wait_recv()
    left = lf[0:32].reshape(RANK, LOCAL_ROWS)

    gram = dot(left, left, ((1,), (1,)))
    gp[0] = gram[:, :128].reshape(NY, NX, 8, 128)
    gp[1] = gram[:, 128:].reshape(NY, NX, 8, 128)
    gram_swap = go(gp.at[1 - c], gs, sibling)

    def partial_rows(core, k):
        cols = pl.ds(pl.multiple_of(core * HALF + k, 128), CHUNK)
        block = dot(left, buf[:, cols], ((1,), (0,)))
        mp[core, :, :, :, pl.ds(k, CHUNK)] = block.reshape(NY, NX, 8, CHUNK)

    rows_swap = []
    for k in range(0, HALF, CHUNK):
        partial_rows(1 - c, k)
        cols = pl.ds(k, CHUNK)
        rows_swap.append(go(mp.at[1 - c, :, :, :, cols], ms.at[:, :, :, cols], sibling))
    gram_swap.wait_recv()
    gs[...] = gs[...] + gp[c]
    gram_y = [go(gs.at[wrap(y + e, NY)], gr.at[e - 1], at(dy=e)) for e in INWARD]
    for k in range(0, HALF, CHUNK):
        partial_rows(c, k)
    for i, k in enumerate(range(0, HALF, CHUNK)):
        rows_swap[i].wait_recv()
        cols = pl.ds(k, CHUNK)
        ms[:, :, :, cols] = ms[:, :, :, cols] + mp[c, :, :, :, cols]

    cols_a, cols_b = pl.ds(0, CUT), pl.ds(CUT, REST)
    scatter_a = [go(ms.at[wrap(y + e, NY), :, :, cols_a], ra.at[e - 1], at(dy=e)) for e in INWARD]
    scatter_b = {}
    for e in INWARD + (0,):
        row = wrap(y + e, NY)
        scatter_b[e] = [
            go(ms.at[row, wrap(x + g, NX), :, cols_b], rb.at[e, g - 1], at(dx=g)) for g in range(1, NX)
        ]

    def gram_sum_y():
        for copy in gram_y:
            copy.wait_recv()
        part = gs[y]
        for e in range(1, NY):
            part = part + gr[e - 1]
        gsum[...] = part
        return [go(gsum.at[wrap(x + g, NX)], gr2.at[g - 1], at(dx=g)) for g in range(1, NX)]

    def gram_sum_x(copies):
        for copy in copies:
            copy.wait_recv()
        part = gsum[x]
        for g in range(1, NX):
            part = part + gr2[g - 1]
        gg[c, y, x] = part
        own = gg.at[c, y, x]
        return [go(own, own, at(dx=g)) for g in range(1, NX)]

    def gram_spread_y(copies):
        for copy in copies:
            copy.wait_recv()
        line = gg.at[c, y]
        return [go(line, line, at(dy=e)) for e in INWARD]

    def gram_hand(copies):
        for copy in copies:
            copy.wait_recv()
        return go(gg.at[c], gg.at[c], sibling)

    def sum_b(e):
        for copy in scatter_b[e]:
            copy.wait_recv()
        part = ms[wrap(y + e, NY), x, :, cols_b]
        for g in range(1, NX):
            part = part + rb[e, g - 1]
        return part

    second_b = []

    def relay_b(e):
        sb[e - 1] = sum_b(e)
        second_b.append(go(sb.at[e - 1], rb2.at[e - 1], at(dy=e)))

    gram_copies = gram_sum_y()
    for e in INWARD[:3]:
        relay_b(e)
    gram_copies = gram_sum_x(gram_copies)
    for e in INWARD[3:5]:
        relay_b(e)
    gram_copies = gram_spread_y(gram_copies)
    for e in INWARD[5:]:
        relay_b(e)
    for copy in scatter_a:
        copy.wait_recv()
    part = ms[y, :, :, cols_a]
    for e in range(1, NY):
        part = part + ra[e - 1]
    sa[...] = part
    second_a = [go(sa.at[wrap(x + g, NX)], ra2.at[g - 1], at(dx=g)) for g in range(1, NX)]
    part_b = sum_b(0)
    gram_copy = gram_hand(gram_copies)
    for copy in second_b:
        copy.wait_recv()
    for e in range(1, NY):
        part_b = part_b + rb2[e - 1]
    mg[c, y, x, :, cols_b] = part_b
    for copy in second_a:
        copy.wait_recv()
    part = sa[x]
    for g in range(1, NX):
        part = part + ra2[g - 1]
    mg[c, y, x, :, cols_a] = part

    gather = Gather(mg)
    gather.start()
    gram_copy.wait_recv()
    work[:, :128] = gg[0].reshape(RANK, 128)
    work[:, 128:] = gg[1].reshape(RANK, 128)

    def factor(first, last):
        def body(k, carry):
            factor_step(work, k)
            return carry

        lax.fori_loop(first, last, body, 0)

    factor(0, 5)
    gather.pass_b(1)
    gather.pass_b(7)
    factor(5, 7)
    gather.pass_a()
    gather.pass_b(2)
    gather.pass_b(6)
    factor(7, 9)
    gather.pass_b(3)
    gather.pass_b(5)
    factor(9, 11)
    gather.pass_b(4)
    gather.hand_b(0)
    factor(11, 13)
    gather.hand_b(1)
    gather.hand_b(7)
    factor(13, 15)
    gather.hand_b(2)
    gather.hand_b(6)
    factor(15, 16)
    r = lax.broadcasted_iota(jnp.int32, (RANK, RANK), 0)
    l = lax.broadcasted_iota(jnp.int32, (RANK, RANK), 1)
    inverse = jnp.where(l <= r, work[...], 0.0)
    work[...] = inverse
    basis = dot(left, inverse, ((0,), (1,)))
    for e in OUTWARD[4:]:
        gather.hand_b(e)
    gather.hand_a()

    def right_rows(core, squares):
        def body(i, squares):
            k = pl.multiple_of(i * CHUNK, 128)
            block = dot(work[...], mg[core, :, :, :, pl.ds(k, CHUNK)].reshape(RANK, CHUNK), ((1,), (0,)))
            rr[:, pl.ds(pl.multiple_of(core * HALF + k, 128), CHUNK)] = block
            for t in range(0, CHUNK, 128):
                squares = squares + block[:, t : t + 128] * block[:, t : t + 128]
            return squares

        return lax.fori_loop(0, HALF // CHUNK, body, squares)

    squares = right_rows(c, jnp.zeros((RANK, 128), f32))
    gather.finish()
    squares = right_rows(1 - c, squares)
    sq[...] = dot(jnp.ones((8, 128), f32), squares, ((1,), (1,)))
    parts = [go(sq, sqr.at[e - 1], at(dz=e)) for e in range(1, NZ)]

    basis16 = basis.astype(bf16)

    def momentum_body(i, carry):
        cols = pl.ds(pl.multiple_of(i * CHUNK, 128), CHUNK)
        product = dot(basis16, rr[:, cols].astype(bf16), ((1,), (0,)), None)
        nm[:, cols] = buf[:, cols] - (1.0 - decay_rate) * product
        return carry

    lax.fori_loop(0, LOCAL // CHUNK, momentum_body, 0)
    for copy in parts:
        copy.wait_recv()
    norm = sq[...]
    for e in range(1, NZ):
        norm = norm + sqr[e - 1]
    inverse_norm = 1.0 / (jnp.sqrt(norm) + norm_eps)
    scaled = basis * (math.sqrt(ROWS * COLS / RANK) * inverse_norm[0:1, :])
    s1 = scaled.astype(bf16)
    s2 = (scaled - s1.astype(f32)).astype(bf16)

    def update_body(i, carry):
        cols = pl.ds(pl.multiple_of(i * CHUNK, 128), CHUNK)
        block = rr[:, cols]
        b1 = block.astype(bf16)
        b2 = (block - b1.astype(f32)).astype(bf16)
        dims = ((1,), (0,))
        product = dot(s1, b1, dims, None) + (dot(s1, b2, dims, None) + dot(s2, b1, dims, None))
        up[:, cols] = product.astype(bf16)
        return carry

    lax.fori_loop(0, LOCAL // CHUNK, update_body, 0)
    chip = y * NX + x
    eight = rr[pl.ds(pl.multiple_of(chip * 8, 8), 8), :]
    r = lax.broadcasted_iota(jnp.int32, (8, RANK), 0)
    l = lax.broadcasted_iota(jnp.int32, (8, RANK), 1)
    own = jnp.sum(jnp.where(l == r + chip * 8, inverse_norm, 0.0), axis=1, keepdims=True)
    eight = eight * own
    nf[...] = jnp.where(c == 0, eight[0:4, :], eight[4:8, :])

    for copy in started:
        copy.wait_send()


def shards(momentum, gradient, right_factor):
    vmem = pl.BlockSpec(memory_space=pltpu.VMEM)
    scratch = [
        (LOCAL_ROWS, LOCAL),
        (2, NY, NX, 8, HALF),
        (4, HALF),
        (36, 8, LOCAL_ROWS),
        (NZ - 1, 3, 8, LOCAL_ROWS),
        (36, 8, LOCAL_ROWS),
        (2, NY, NX, 8, 128),
        (NY, NX, 8, 128),
        (NY - 1, NX, 8, 128),
        (NX, 8, 128),
        (NX - 1, 8, 128),
        (2, NY, NX, 8, 128),
        (2, NY, NX, 8, HALF),
        (NY, NX, 8, HALF),
        (NY - 1, NX, 8, CUT),
        (NX, 8, CUT),
        (NX - 1, 8, CUT),
        (NY, NX - 1, 8, REST),
        (NY - 1, 8, REST),
        (NY - 1, 8, REST),
        (2, NY, NX, 8, HALF),
        (RANK, RANK),
        (RANK, LOCAL),
        (8, RANK),
        (NZ - 1, 8, RANK),
    ]
    return pl.pallas_call(
        kernel,
        out_shape=(
            jax.ShapeDtypeStruct((LOCAL_ROWS, LOCAL), f32),
            jax.ShapeDtypeStruct((LOCAL_ROWS, LOCAL), bf16),
            jax.ShapeDtypeStruct((4, LOCAL), f32),
        ),
        in_specs=[vmem] * 3,
        out_specs=(vmem,) * 3,
        scratch_shapes=[pltpu.VMEM(shape, f32) for shape in scratch]
        + [pltpu.SemaphoreType.DMA((COPIES,)), pltpu.SemaphoreType.DMA((COPIES,))],
        compiler_params=pltpu.CompilerParams(collective_id=0, has_side_effects=True, vmem_limit_bytes=VMEM_LIMIT),
    )(momentum, gradient, right_factor)


def solution(mesh):
    spec = P("fsdp", "tp")
    return jax.shard_map(shards, mesh=mesh, in_specs=(spec,) * 3, out_specs=(spec,) * 3, check_vma=False)
```

time: 739 us -> 121 us (0.16)
  waiting for transfers between devices: 614 us -> 0 us
  Pallas kernels: 0 us -> 114 us
  other arithmetic: 56.9 us -> 0 us
  blocking collectives: 19.9 us -> 0 us
  matrix products: 15.6 us -> 0 us
  between operations: 15.3 us -> 0.65 us
    psum x3 -> x0, waiting for transfers between devices: 514 us -> none  [the longest x1 208 us: shards(): lax.psum(jnp.dot(left_basis.T, buffer, precision=highest), 'fsdp')]
    pallas_call x0 -> x1, Pallas kernels: none -> 114 us  [shards(): pl.pallas_call(kernel, out_shape=(jax.ShapeDtypeStruct((LOCAL_ROWS, LOCAL...]
    all_gather x1 -> x0, waiting for transfers between devices: 100 us -> none  [shards(): lax.all_gather(right_factor, 'fsdp', axis=0, tiled=True)]
    another operation x9 -> x0, other arithmetic: 53.7 us -> none  [the longest x6 34 us: shards(): lower_factor = jnp.linalg.cholesky(gram_total)]
    psum x1 -> x0, blocking collectives: 19.9 us -> none  [shards(): norm_total = lax.psum(squares, 'tp')]
    dot_general x5 -> x0, matrix products: 14.3 us -> none  [the longest x1 4.16 us: shards(): lax.dot_general(buffer, lax.all_gather(right_factor, 'fsdp', axis=0, tile...]
  transfers between devices with their start and end apart: 4 -> 0, of which waited for: 4 -> 0; matrix products, arithmetic and copies ran while one was open for 0% -> 0% of each run, Pallas kernels for 0% -> 0%
where the time goes in v1:
time: 121 us
  Pallas kernels  114 us (94%)
  local copies, waits for them, and re-layouts  5.54 us (5%)
    pallas_call x1, Pallas kernels, shards(): pl.pallas_call(kernel, out_shape=(jax.ShapeDtypeStruct((LOCAL_ROWS, LOCAL...  114 us
    unnamed x9, local copies, waits for them, and re-layouts  5.54 us

profile of v1, /device:TPU:1, one launch (start us, length us, event | category | flops | bytes accessed | tf_op | source)
XLA Modules:
  0.0 120.6 jit_solution(14379246464421874389)
XLA Ops:
  0.6 0.0 copy-start
  0.6 1.3 %copy-done = f32[128,2304]{1,0:T(8,128)S(1)} copy-done((f32[128,2304]{1,0:T(8,128)S(1)}, f32[128,2304]{1,0:T(8,128)}, u32[]{:S(2)}) %copy-start) | copy-done | bytes 1179672
  1.9 0.0 copy-start.1
  1.9 1.1 copy-done.1
  3.0 0.0 copy-start.2
  3.0 0.8 copy-done.2
  3.7 114.4 %shard_map.58 = (f32[128,2304]{1,0:T(8,128)S(1)}, bf16[128,2304]{1,0:T(8,128)(2,1)S(1)}, f32[4,2304]{1,0:T(4,128)S(1)}) custom-call(f32[128,2304]{1,0:T(8,128)S(1)} %copy-done, bf16[128,2304]{1,0:T(8,128)(2,1)S(1)} %copy-done.1, f32[4,2304]{1,0:T(4,128)S(1)} %copy-done.2), custom_call_target="tpu_custom_call" | custom-call | tf_op jit(solution)/shard_map/pallas_call | solution.py:447
  118.2 1.0 copy.9
  119.2 0.8 copy.10
  120.0 0.6 copy.11
Async XLA Ops:
  0.6 1.3 %copy-start = (f32[128,2304]{1,0:T(8,128)S(1)}, f32[128,2304]{1,0:T(8,128)}, u32[]{:S(2)}) copy-start(f32[128,2304]{1,0:T(8,128)} %mom.1) | copy-start | bytes 3538948
  1.9 1.1 copy-start.1
  3.0 0.8 copy-start.2

commit v2 on v1

--- a/solution.py
+++ b/solution.py
@@ -26,12 +26,14 @@
 HALF = LOCAL // 2
 CUT = 256
 REST = HALF - CUT
+PART = 384
 CHUNK = 384
+WIDE = 768
 BLOCK = 16
 OUTWARD = (1, 7, 2, 6, 3, 5, 4)
 INWARD = (4, 3, 5, 2, 6, 1, 7)
 COPIES = 384
-VMEM_LIMIT = 48 << 20
+VMEM_LIMIT = 32 << 20
 
 
 def dot(a, b, dims, precision=HIGHEST):
@@ -85,9 +87,9 @@
 
 
 def kernel(
-    mom, grad, rf, nm, up, nf,
-    buf, rg, sib4, lp, zr, lf, gp, gs, gr, gsum, gr2, gg, mp, ms, ra, sa, ra2, rb, sb, rb2, mg, work, rr, sq, sqr,
-    send, recv,
+    mom_hbm, grad_hbm, rf_hbm, nm, rr, scaled_ref, nf,
+    mom, rf, buf, rg, sib4, lp, zr, lf, gp, gs, gr, gsum, gr2, gg, mp, ms, ra, ra1, sa, ra2, rb, sb, rb2, rb4, mg, work, sq, sqr,
+    grad, send, recv, load,
 ):
     f, z = lax.axis_index("fsdp"), lax.axis_index("tp")
     c, x, y = lax.rem(f, 2), lax.rem(lax.div(f, 2), NX), lax.div(f, 2 * NX)
@@ -112,12 +114,18 @@
         started.append(copy)
         return copy
 
+    loads = [
+        pltpu.make_async_copy(src, dst, load.at[i])
+        for i, (src, dst) in enumerate(((rf_hbm, rf), (mom_hbm, mom), (grad_hbm, grad)))
+    ]
+    for copy in loads:
+        copy.start()
     peers = [sibling] + [at(dx=e) for e in range(1, NX)] + [at(dy=e) for e in range(1, NY)]
     peers += [at(dz=e) for e in range(1, NZ)]
     barrier = pltpu.get_barrier_semaphore()
     for peer in peers:
         pl.semaphore_signal(barrier, inc=1, device_id=peer, device_id_type=MESH)
-    buf[...] = mom[...] + grad[...].astype(f32)
+    loads[0].wait()
     pl.semaphore_wait(barrier, len(peers))
 
     class Gather:
@@ -167,10 +175,13 @@
     rg[c, y, x, 4:8, :] = jnp.where(c == 0, theirs, mine)
     gather = Gather(rg)
     gather.start()
-    gather.pass_b(1)
-    gather.pass_b(7)
+    for copy in loads[1:]:
+        copy.wait()
+    buf[...] = mom[...] + grad[...].astype(f32)
+    for e in OUTWARD[:4]:
+        gather.pass_b(e)
     gather.pass_a()
-    for e in OUTWARD[2:]:
+    for e in OUTWARD[4:]:
         gather.pass_b(e)
     for e in (0,) + OUTWARD:
         gather.hand_b(e)
@@ -223,7 +234,7 @@
         rows_swap.append(go(mp.at[1 - c, :, :, :, cols], ms.at[:, :, :, cols], sibling))
     gram_swap.wait_recv()
     gs[...] = gs[...] + gp[c]
-    gram_y = [go(gs.at[wrap(y + e, NY)], gr.at[e - 1], at(dy=e)) for e in INWARD]
+    gram_x = [go(gs.at[:, wrap(x + g, NX)], gr.at[g - 1], at(dx=g)) for g in (2, 1, 3)]
     for k in range(0, HALF, CHUNK):
         partial_rows(c, k)
     for i, k in enumerate(range(0, HALF, CHUNK)):
@@ -232,90 +243,141 @@
         ms[:, :, :, cols] = ms[:, :, :, cols] + mp[c, :, :, :, cols]
 
     cols_a, cols_b = pl.ds(0, CUT), pl.ds(CUT, REST)
-    scatter_a = [go(ms.at[wrap(y + e, NY), :, :, cols_a], ra.at[e - 1], at(dy=e)) for e in INWARD]
-    scatter_b = {}
-    for e in INWARD + (0,):
-        row = wrap(y + e, NY)
-        scatter_b[e] = [
-            go(ms.at[row, wrap(x + g, NX), :, cols_b], rb.at[e, g - 1], at(dx=g)) for g in range(1, NX)
-        ]
-
-    def gram_sum_y():
-        for copy in gram_y:
+    low, high = pl.ds(CUT, PART), pl.ds(CUT + PART, REST - PART)
+
+    def line_a(e, first=0, count=NX):
+        return ms.at[wrap(y + e, NY), pl.ds(first, count), :, cols_a]
+
+    def block_b(e, dx):
+        return ms.at[wrap(y + e, NY), wrap(x + dx, NX), :, cols_b]
+
+    near_a = [
+        go(line_a(3), ra1.at[0], at(dy=1)),
+        go(line_a(5), ra1.at[1], at(dy=-1)),
+        go(line_a(4, 0, 2), ra1.at[2, pl.ds(0, 2)], at(dy=2)),
+        go(line_a(4, 2, 2), ra1.at[3, pl.ds(2, 2)], at(dy=-2)),
+    ]
+    order = (4, 3, 5, 2, 6, 1, 7, 0)
+    first_b, direct_b, relay_b = {}, {}, {}
+    for e in order:
+        step = 1 if e % 2 == 0 else -1
+        first_b[e] = go(block_b(e, 2), rb.at[e, 0], at(dx=step))
+        direct_b[e] = go(block_b(e, -step), rb.at[e, 1], at(dx=-step))
+    far_a = {e: go(line_a(e), ra.at[e - 1], at(dy=e)) for e in (1, 7)}
+
+    def relay_x(e):
+        step = 1 if e % 2 == 0 else -1
+        first_b[e].wait_recv()
+        block = block_b(e, step)
+        block[...] = block[...] + rb[e, 0]
+        relay_b[e] = go(block, rb.at[e, 2], at(dx=step))
+
+    def relay_a():
+        for copy in near_a:
             copy.wait_recv()
-        part = gs[y]
-        for e in range(1, NY):
-            part = part + gr[e - 1]
+        forward, back = wrap(y + 2, NY), wrap(y - 2, NY)
+        ms[forward, :, :, cols_a] = ms[forward, :, :, cols_a] + ra1[0]
+        ms[forward, 0:2, :, cols_a] = ms[forward, 0:2, :, cols_a] + ra1[2, 0:2]
+        ms[back, :, :, cols_a] = ms[back, :, :, cols_a] + ra1[1]
+        ms[back, 2:4, :, cols_a] = ms[back, 2:4, :, cols_a] + ra1[3, 2:4]
+        far_a.update({e: go(line_a(e), ra.at[e - 1], at(dy=e)) for e in (2, 6)})
+
+    def sum_a():
+        for e in (1, 7, 2, 6):
+            far_a[e].wait_recv()
+        sa[...] = ms[y, :, :, cols_a] + ra[0] + ra[6] + ra[1] + ra[5]
+        return [go(sa.at[wrap(x + g, NX)], ra2.at[g - 1], at(dx=g)) for g in (2, 1, 3)]
+
+    def sum_b(e):
+        direct_b[e].wait_recv()
+        relay_b[e].wait_recv()
+        return ms[wrap(y + e, NY), x, :, cols_b] + rb[e, 1] + rb[e, 2]
+
+    last_b, quarter = [], []
+
+    def send_y(e):
+        sb[e] = sum_b(e)
+        if e == 4:
+            for part, way in ((pl.ds(0, PART), 2), (pl.ds(PART, REST - PART), -2)):
+                quarter.append(go(sb.at[4, :, part], rb4.at[:, part], at(dy=way)))
+        else:
+            last_b.append(go(sb.at[e], rb2.at[e - 1], at(dy=e)))
+
+    def send_two():
+        for copy in quarter:
+            copy.wait_recv()
+        total = sum_b(2)
+        sb[2, :, :PART] = total[:, :PART] + rb4[:, :PART]
+        sb[2, :, PART:] = total[:, PART:]
+        last_b.append(go(sb.at[2], rb2.at[1], at(dy=2)))
+        total = sum_b(6)
+        sb[6, :, :PART] = total[:, :PART]
+        sb[6, :, PART:] = total[:, PART:] + rb4[:, PART:]
+        last_b.append(go(sb.at[6], rb2.at[5], at(dy=6)))
+
+    def gram_sum_x():
+        for copy in gram_x:
+            copy.wait_recv()
+        part = gs[:, x]
+        for g in range(1, NX):
+            part = part + gr[g - 1]
         gsum[...] = part
-        return [go(gsum.at[wrap(x + g, NX)], gr2.at[g - 1], at(dx=g)) for g in range(1, NX)]
-
-    def gram_sum_x(copies):
+        return [go(gsum.at[wrap(y + e, NY)], gr2.at[e - 1], at(dy=e)) for e in INWARD]
+
+    def gram_sum_y(copies):
         for copy in copies:
             copy.wait_recv()
-        part = gsum[x]
-        for g in range(1, NX):
-            part = part + gr2[g - 1]
+        part = gsum[y]
+        for e in range(1, NY):
+            part = part + gr2[e - 1]
         gg[c, y, x] = part
         own = gg.at[c, y, x]
-        return [go(own, own, at(dx=g)) for g in range(1, NX)]
-
-    def gram_spread_y(copies):
+        return [go(own, own, at(dy=e)) for e in INWARD]
+
+    def gram_spread_x(copies):
         for copy in copies:
             copy.wait_recv()
-        line = gg.at[c, y]
-        return [go(line, line, at(dy=e)) for e in INWARD]
+        line = gg.at[c, :, x]
+        return [go(line, line, at(dx=g)) for g in (2, 1, 3)]
 
     def gram_hand(copies):
         for copy in copies:
             copy.wait_recv()
         return go(gg.at[c], gg.at[c], sibling)
 
-    def sum_b(e):
-        for copy in scatter_b[e]:
-            copy.wait_recv()
-        part = ms[wrap(y + e, NY), x, :, cols_b]
-        for g in range(1, NX):
-            part = part + rb[e, g - 1]
-        return part
-
-    second_b = []
-
-    def relay_b(e):
-        sb[e - 1] = sum_b(e)
-        second_b.append(go(sb.at[e - 1], rb2.at[e - 1], at(dy=e)))
-
-    gram_copies = gram_sum_y()
-    for e in INWARD[:3]:
-        relay_b(e)
-    gram_copies = gram_sum_x(gram_copies)
-    for e in INWARD[3:5]:
-        relay_b(e)
-    gram_copies = gram_spread_y(gram_copies)
-    for e in INWARD[5:]:
-        relay_b(e)
-    for copy in scatter_a:
-        copy.wait_recv()
-    part = ms[y, :, :, cols_a]
-    for e in range(1, NY):
-        part = part + ra[e - 1]
-    sa[...] = part
-    second_a = [go(sa.at[wrap(x + g, NX)], ra2.at[g - 1], at(dx=g)) for g in range(1, NX)]
+    gram_copies = gram_sum_x()
+    for e in order[:5]:
+        relay_x(e)
+    relay_a()
+    gram_copies = gram_sum_y(gram_copies)
+    for e in order[5:]:
+        relay_x(e)
+    for e in (4, 3, 5):
+        send_y(e)
+    gram_copies = gram_spread_x(gram_copies)
+    for e in (1, 7):
+        send_y(e)
+    second_a = sum_a()
+    send_two()
     part_b = sum_b(0)
-    gram_copy = gram_hand(gram_copies)
-    for copy in second_b:
-        copy.wait_recv()
-    for e in range(1, NY):
-        part_b = part_b + rb2[e - 1]
-    mg[c, y, x, :, cols_b] = part_b
     for copy in second_a:
         copy.wait_recv()
     part = sa[x]
     for g in range(1, NX):
         part = part + ra2[g - 1]
     mg[c, y, x, :, cols_a] = part
+    for copy in last_b:
+        copy.wait_recv()
+    for e in (1, 7, 2, 6, 3, 5):
+        part_b = part_b + rb2[e - 1]
+    mg[c, y, x, :, cols_b] = part_b
 
     gather = Gather(mg)
     gather.start()
+    gram_copy = gram_hand(gram_copies)
+    for e in OUTWARD[:4]:
+        gather.pass_b(e)
+    gather.pass_a()
     gram_copy.wait_recv()
     work[:, :128] = gg[0].reshape(RANK, 128)
     work[:, 128:] = gg[1].reshape(RANK, 128)
@@ -327,34 +389,31 @@
 
         lax.fori_loop(first, last, body, 0)
 
-    factor(0, 5)
-    gather.pass_b(1)
-    gather.pass_b(7)
-    factor(5, 7)
-    gather.pass_a()
-    gather.pass_b(2)
-    gather.pass_b(6)
-    factor(7, 9)
+    factor(0, 1)
     gather.pass_b(3)
     gather.pass_b(5)
-    factor(9, 11)
+    factor(1, 2)
     gather.pass_b(4)
+    factor(2, 6)
     gather.hand_b(0)
-    factor(11, 13)
+    factor(6, 8)
     gather.hand_b(1)
     gather.hand_b(7)
-    factor(13, 15)
+    factor(8, 10)
     gather.hand_b(2)
     gather.hand_b(6)
+    factor(10, 13)
+    gather.hand_b(3)
+    gather.hand_b(5)
+    factor(13, 15)
+    gather.hand_b(4)
+    gather.hand_a()
     factor(15, 16)
     r = lax.broadcasted_iota(jnp.int32, (RANK, RANK), 0)
     l = lax.broadcasted_iota(jnp.int32, (RANK, RANK), 1)
     inverse = jnp.where(l <= r, work[...], 0.0)
     work[...] = inverse
     basis = dot(left, inverse, ((0,), (1,)))
-    for e in OUTWARD[4:]:
-        gather.hand_b(e)
-    gather.hand_a()
 
     def right_rows(core, squares):
         def body(i, squares):
@@ -389,20 +448,7 @@
         norm = norm + sqr[e - 1]
     inverse_norm = 1.0 / (jnp.sqrt(norm) + norm_eps)
     scaled = basis * (math.sqrt(ROWS * COLS / RANK) * inverse_norm[0:1, :])
-    s1 = scaled.astype(bf16)
-    s2 = (scaled - s1.astype(f32)).astype(bf16)
-
-    def update_body(i, carry):
-        cols = pl.ds(pl.multiple_of(i * CHUNK, 128), CHUNK)
-        block = rr[:, cols]
-        b1 = block.astype(bf16)
-        b2 = (block - b1.astype(f32)).astype(bf16)
-        dims = ((1,), (0,))
-        product = dot(s1, b1, dims, None) + (dot(s1, b2, dims, None) + dot(s2, b1, dims, None))
-        up[:, cols] = product.astype(bf16)
-        return carry
-
-    lax.fori_loop(0, LOCAL // CHUNK, update_body, 0)
+    scaled_ref[...] = scaled
     chip = y * NX + x
     eight = rr[pl.ds(pl.multiple_of(chip * 8, 8), 8), :]
     r = lax.broadcasted_iota(jnp.int32, (8, RANK), 0)
@@ -415,9 +461,33 @@
         copy.wait_send()
 
 
+def finish(nm, rr, scaled, nf, nm_out, up_out, nf_out, up, done):
+    copies = [pltpu.make_async_copy(nm, nm_out, done.at[0]), pltpu.make_async_copy(nf, nf_out, done.at[1])]
+    for copy in copies:
+        copy.start()
+    s = scaled[...]
+    s1 = s.astype(bf16)
+    s2 = (s - s1.astype(f32)).astype(bf16)
+    for i in range(LOCAL // WIDE):
+        cols = pl.ds(i * WIDE, WIDE)
+        block = rr[:, cols]
+        b1 = block.astype(bf16)
+        b2 = (block - b1.astype(f32)).astype(bf16)
+        dims = ((1,), (0,))
+        product = dot(s1, b1, dims, None) + (dot(s1, b2, dims, None) + dot(s2, b1, dims, None))
+        up[:, cols] = product.astype(bf16)
+        copies.append(pltpu.make_async_copy(up.at[:, cols], up_out.at[:, cols], done.at[2 + i]))
+        copies[-1].start()
+    for copy in copies:
+        copy.wait()
+
+
 def shards(momentum, gradient, right_factor):
     vmem = pl.BlockSpec(memory_space=pltpu.VMEM)
+    hbm = pl.BlockSpec(memory_space=pltpu.HBM)
     scratch = [
+        (LOCAL_ROWS, LOCAL),
+        (4, LOCAL),
         (LOCAL_ROWS, LOCAL),
         (2, NY, NX, 8, HALF),
         (4, HALF),
@@ -426,37 +496,53 @@
         (36, 8, LOCAL_ROWS),
         (2, NY, NX, 8, 128),
         (NY, NX, 8, 128),
-        (NY - 1, NX, 8, 128),
-        (NX, 8, 128),
-        (NX - 1, 8, 128),
+        (NX - 1, NY, 8, 128),
+        (NY, 8, 128),
+        (NY - 1, 8, 128),
         (2, NY, NX, 8, 128),
         (2, NY, NX, 8, HALF),
         (NY, NX, 8, HALF),
         (NY - 1, NX, 8, CUT),
+        (4, NX, 8, CUT),
         (NX, 8, CUT),
         (NX - 1, 8, CUT),
-        (NY, NX - 1, 8, REST),
+        (NY, 3, 8, REST),
+        (NY, 8, REST),
         (NY - 1, 8, REST),
-        (NY - 1, 8, REST),
+        (8, REST),
         (2, NY, NX, 8, HALF),
         (RANK, RANK),
-        (RANK, LOCAL),
         (8, RANK),
         (NZ - 1, 8, RANK),
     ]
-    return pl.pallas_call(
+    shape = jax.ShapeDtypeStruct
+    parts = pl.pallas_call(
         kernel,
         out_shape=(
-            jax.ShapeDtypeStruct((LOCAL_ROWS, LOCAL), f32),
-            jax.ShapeDtypeStruct((LOCAL_ROWS, LOCAL), bf16),
-            jax.ShapeDtypeStruct((4, LOCAL), f32),
+            shape((LOCAL_ROWS, LOCAL), f32),
+            shape((RANK, LOCAL), f32),
+            shape((LOCAL_ROWS, RANK), f32),
+            shape((4, LOCAL), f32),
         ),
-        in_specs=[vmem] * 3,
-        out_specs=(vmem,) * 3,
-        scratch_shapes=[pltpu.VMEM(shape, f32) for shape in scratch]
-        + [pltpu.SemaphoreType.DMA((COPIES,)), pltpu.SemaphoreType.DMA((COPIES,))],
+        in_specs=[hbm] * 3,
+        out_specs=(vmem,) * 4,
+        scratch_shapes=[pltpu.VMEM(each, f32) for each in scratch]
+        + [pltpu.VMEM((LOCAL_ROWS, LOCAL), bf16)]
+        + [pltpu.SemaphoreType.DMA((COPIES,)), pltpu.SemaphoreType.DMA((COPIES,)), pltpu.SemaphoreType.DMA((3,))],
         compiler_params=pltpu.CompilerParams(collective_id=0, has_side_effects=True, vmem_limit_bytes=VMEM_LIMIT),
-    )(momentum, gradient, right_factor)
+    )(*[pltpu.with_memory_space_constraint(a, pltpu.HBM) for a in (momentum, gradient, right_factor)])
+    return pl.pallas_call(
+        finish,
+        out_shape=(
+            shape((LOCAL_ROWS, LOCAL), f32),
+            shape((LOCAL_ROWS, LOCAL), bf16),
+            shape((4, LOCAL), f32),
+        ),
+        in_specs=[vmem] * 4,
+        out_specs=(hbm,) * 3,
+        scratch_shapes=[pltpu.VMEM((LOCAL_ROWS, LOCAL), bf16), pltpu.SemaphoreType.DMA((2 + LOCAL // WIDE,))],
+        compiler_params=pltpu.CompilerParams(vmem_limit_bytes=16 << 20),
+    )(*parts)
 
 
 def solution(mesh):

time: 121 us -> 113 us (0.934)
  local copies, waits for them, and re-layouts: 5.54 us -> 0 us
  Pallas kernels: 114 us -> 112 us
    unnamed x9 -> x0, local copies, waits for them, and re-layouts: 5.54 us -> none
    pallas_call x1 -> x2, Pallas kernels: 114 us -> 112 us  [the longest x1 110 us: shards(): pl.pallas_call(kernel, out_shape=(shape((LOCAL_ROWS, LOCAL), f32), shape(...]
where the time goes in v2:
time: 113 us; the launch traced here: 112 us
  Pallas kernels  112 us (99%)
    pallas_call x1, Pallas kernels, shards(): pl.pallas_call(kernel, out_shape=(shape((LOCAL_ROWS, LOCAL), f32), shape(...  110 us

profile of v2, /device:TPU:1, one launch (start us, length us, event | category | flops | bytes accessed | tf_op | source)
XLA Modules:
  0.0 112.5 jit_solution(9857394231701704788)
XLA Ops:
  0.6 110.4 %shard_map.58 = (f32[128,2304]{1,0:T(8,128)S(1)}, f32[256,2304]{1,0:T(8,128)S(1)}, f32[128,256]{1,0:T(8,128)S(1)}, f32[4,2304]{1,0:T(4,128)S(1)}) custom-call(f32[128,2304]{1,0:T(8,128)} %mom_hbm.1, bf16[128,2304]{1,0:T(8,128)(2,1)} %grad_hbm.1, f32[4,2304]{1,0:T(4,128)} %rf_hbm.1), custom_call_target="tpu_custom_call" | custom-call | tf_op jit(solution)/shard_map/pallas_call | solution.py:519
  111.0 1.5 %shard_map.59 = (f32[128,2304]{1,0:T(8,128)}, bf16[128,2304]{1,0:T(8,128)(2,1)}, f32[4,2304]{1,0:T(4,128)}) custom-call(f32[128,2304]{1,0:T(8,128)S(1)} %get-tuple-element.7.nm, f32[256,2304]{1,0:T(8,128)S(1)} %get-tuple-element.8.rr, f32[128,256]{1,0:T(8,128)S(1)} %get-tuple-element.9.scaled, f32[4,2304]{1,0:T(4,128)S(1)} %get-tuple-element.10.nf), custom_call_target="tpu_custom_call" | custom-call | tf_op jit(solution)/shard_map/pallas_call | solution.py:534

commit v3 on v2

--- a/solution.py
+++ b/solution.py
@@ -32,6 +32,7 @@
 BLOCK = 16
 OUTWARD = (1, 7, 2, 6, 3, 5, 4)
 INWARD = (4, 3, 5, 2, 6, 1, 7)
+AROUND = (6, 5, 7, 4, 8, 3, 9, 2, 10, 1, 11)
 COPIES = 384
 VMEM_LIMIT = 32 << 20
 
@@ -144,24 +145,21 @@
             for copy in self.ax:
                 copy.wait_recv()
             line = self.half.at[y, :, :, self.cols_a]
-            self.ay = [go(line, line, at(dy=e)) for e in INWARD]
+            self.ay = {e: go(line, line, at(dy=e)) for e in INWARD}
+            self.given = []
 
         def pass_b(self, e):
             self.by[e].wait_recv()
             block = self.half.at[wrap(y - e, NY), x, :, self.cols_b]
             self.bx[e] = [go(block, block, at(dx=g)) for g in range(1, NX)]
 
-        def hand_b(self, e):
+        def hand(self, e):
             for copy in self.bx[e]:
                 copy.wait_recv()
-            line = self.half.at[wrap(y - e, NY), :, :, self.cols_b]
-            self.given = getattr(self, "given", []) + [go(line, line, sibling)]
-
-        def hand_a(self):
-            for copy in self.ay:
-                copy.wait_recv()
-            part = self.half.at[:, :, :, self.cols_a]
-            self.given.append(go(part, part, sibling))
+            if e:
+                self.ay[e].wait_recv()
+            line = self.half.at[wrap(y - e, NY)]
+            self.given.append(go(line, line, sibling))
 
         def finish(self):
             for copy in self.given:
@@ -184,8 +182,7 @@
     for e in OUTWARD[4:]:
         gather.pass_b(e)
     for e in (0,) + OUTWARD:
-        gather.hand_b(e)
-    gather.hand_a()
+        gather.hand(e)
 
     def partial_left(core, total):
         def body(i, total):
@@ -203,16 +200,20 @@
     lp[0:32] = total.reshape(32, 8, LOCAL_ROWS)
     lp[32:36] = jnp.zeros((4, 8, LOCAL_ROWS), f32)
     own_tiles = pl.ds(z * 3, 3)
+    gathered = list(started)
     parts = []
-    for e in range(1, NZ):
+    for e in AROUND:
         parts.append(go(lp.at[pl.ds(wrap(z + e, NZ) * 3, 3)], zr.at[e - 1], at(dz=e)))
+    for copy in gathered:
+        copy.wait_send()
+    del started[: len(gathered)]
     for copy in parts:
         copy.wait_recv()
     tiles = lp[own_tiles]
     for e in range(1, NZ):
         tiles = tiles + zr[e - 1]
     lf[own_tiles] = tiles
-    parts = [go(lf.at[own_tiles], lf.at[own_tiles], at(dz=e)) for e in range(1, NZ)]
+    parts = [go(lf.at[own_tiles], lf.at[own_tiles], at(dz=e)) for e in AROUND]
     for copy in parts:
         copy.wait_recv()
     left = lf[0:32].reshape(RANK, LOCAL_ROWS)
@@ -222,9 +223,13 @@
     gp[1] = gram[:, 128:].reshape(NY, NX, 8, 128)
     gram_swap = go(gp.at[1 - c], gs, sibling)
 
+    l1, l2, l3 = split3(left)
+    stacked = jnp.concatenate([l1, l1, l2, l2, l1, l3], axis=1)
+
     def partial_rows(core, k):
         cols = pl.ds(pl.multiple_of(core * HALF + k, 128), CHUNK)
-        block = dot(left, buf[:, cols], ((1,), (0,)))
+        b1, b2, b3 = split3(buf[:, cols])
+        block = dot(stacked, jnp.concatenate([b1, b2, b1, b2, b3, b1], axis=0), ((1,), (0,)), None)
         mp[core, :, :, :, pl.ds(k, CHUNK)] = block.reshape(NY, NX, 8, CHUNK)
 
     rows_swap = []
@@ -251,20 +256,12 @@
     def block_b(e, dx):
         return ms.at[wrap(y + e, NY), wrap(x + dx, NX), :, cols_b]
 
-    near_a = [
-        go(line_a(3), ra1.at[0], at(dy=1)),
-        go(line_a(5), ra1.at[1], at(dy=-1)),
-        go(line_a(4, 0, 2), ra1.at[2, pl.ds(0, 2)], at(dy=2)),
-        go(line_a(4, 2, 2), ra1.at[3, pl.ds(2, 2)], at(dy=-2)),
-    ]
     order = (4, 3, 5, 2, 6, 1, 7, 0)
     first_b, direct_b, relay_b = {}, {}, {}
     for e in order:
         step = 1 if e % 2 == 0 else -1
         first_b[e] = go(block_b(e, 2), rb.at[e, 0], at(dx=step))
         direct_b[e] = go(block_b(e, -step), rb.at[e, 1], at(dx=-step))
-    far_a = {e: go(line_a(e), ra.at[e - 1], at(dy=e)) for e in (1, 7)}
-
     def relay_x(e):
         step = 1 if e % 2 == 0 else -1
         first_b[e].wait_recv()
@@ -346,17 +343,22 @@
         return go(gg.at[c], gg.at[c], sibling)
 
     gram_copies = gram_sum_x()
+    near_a = [
+        go(line_a(3), ra1.at[0], at(dy=1)),
+        go(line_a(5), ra1.at[1], at(dy=-1)),
+        go(line_a(4, 0, 2), ra1.at[2, pl.ds(0, 2)], at(dy=2)),
+        go(line_a(4, 2, 2), ra1.at[3, pl.ds(2, 2)], at(dy=-2)),
+    ]
+    far_a = {e: go(line_a(e), ra.at[e - 1], at(dy=e)) for e in (1, 7)}
     for e in order[:5]:
         relay_x(e)
-    relay_a()
     gram_copies = gram_sum_y(gram_copies)
     for e in order[5:]:
         relay_x(e)
-    for e in (4, 3, 5):
+    relay_a()
+    for e in (4, 3, 5, 1, 7):
         send_y(e)
     gram_copies = gram_spread_x(gram_copies)
-    for e in (1, 7):
-        send_y(e)
     second_a = sum_a()
     send_two()
     part_b = sum_b(0)
@@ -375,9 +377,7 @@
     gather = Gather(mg)
     gather.start()
     gram_copy = gram_hand(gram_copies)
-    for e in OUTWARD[:4]:
-        gather.pass_b(e)
-    gather.pass_a()
+    gather.pass_b(1)
     gram_copy.wait_recv()
     work[:, :128] = gg[0].reshape(RANK, 128)
     work[:, 128:] = gg[1].reshape(RANK, 128)
@@ -389,36 +389,39 @@
 
         lax.fori_loop(first, last, body, 0)
 
+    gather.pass_b(7)
     factor(0, 1)
+    gather.pass_b(2)
+    gather.pass_b(6)
+    gather.pass_a()
+    factor(1, 3)
     gather.pass_b(3)
     gather.pass_b(5)
-    factor(1, 2)
+    factor(3, 4)
     gather.pass_b(4)
-    factor(2, 6)
-    gather.hand_b(0)
-    factor(6, 8)
-    gather.hand_b(1)
-    gather.hand_b(7)
-    factor(8, 10)
-    gather.hand_b(2)
-    gather.hand_b(6)
-    factor(10, 13)
-    gather.hand_b(3)
-    gather.hand_b(5)
+    factor(4, 9)
+    gather.hand(0)
+    factor(9, 11)
+    gather.hand(1)
+    gather.hand(7)
+    factor(11, 13)
+    gather.hand(2)
+    gather.hand(6)
     factor(13, 15)
-    gather.hand_b(4)
-    gather.hand_a()
+    gather.hand(3)
+    gather.hand(5)
     factor(15, 16)
+    gather.hand(4)
     r = lax.broadcasted_iota(jnp.int32, (RANK, RANK), 0)
     l = lax.broadcasted_iota(jnp.int32, (RANK, RANK), 1)
-    inverse = jnp.where(l <= r, work[...], 0.0)
-    work[...] = inverse
-    basis = dot(left, inverse, ((0,), (1,)))
+    work[...] = jnp.where(l <= r, work[...], 0.0)
 
     def right_rows(core, squares):
         def body(i, squares):
             k = pl.multiple_of(i * CHUNK, 128)
-            block = dot(work[...], mg[core, :, :, :, pl.ds(k, CHUNK)].reshape(RANK, CHUNK), ((1,), (0,)))
+            rows = mg[core, :, :, :, pl.ds(k, CHUNK)].reshape(RANK, CHUNK)
+            top = dot(work[:128, :128], rows[:128], ((1,), (0,)))
+            block = jnp.concatenate([top, dot(work[128:, :], rows, ((1,), (0,)))], axis=0)
             rr[:, pl.ds(pl.multiple_of(core * HALF + k, 128), CHUNK)] = block
             for t in range(0, CHUNK, 128):
                 squares = squares + block[:, t : t + 128] * block[:, t : t + 128]
@@ -430,8 +433,12 @@
     gather.finish()
     squares = right_rows(1 - c, squares)
     sq[...] = dot(jnp.ones((8, 128), f32), squares, ((1,), (1,)))
-    parts = [go(sq, sqr.at[e - 1], at(dz=e)) for e in range(1, NZ)]
-
+    earlier = list(started)
+    parts = [go(sq, sqr.at[e - 1], at(dz=e)) for e in AROUND]
+
+    for copy in earlier:
+        copy.wait_send()
+    basis = dot(left, work[...], ((0,), (1,)))
     basis16 = basis.astype(bf16)
 
     def momentum_body(i, carry):
@@ -456,8 +463,7 @@
     own = jnp.sum(jnp.where(l == r + chip * 8, inverse_norm, 0.0), axis=1, keepdims=True)
     eight = eight * own
     nf[...] = jnp.where(c == 0, eight[0:4, :], eight[4:8, :])
-
-    for copy in started:
+    for copy in parts:
         copy.wait_send()
 
 

time: 113 us -> 109 us (0.965)
  Pallas kernels: 112 us -> 108 us
    pallas_call x1, Pallas kernels: 110 us -> 106 us  [shards(): pl.pallas_call(kernel, out_shape=(shape((LOCAL_ROWS, LOCAL), f32), shape(...]
where the time goes in v3:
time: 109 us; the launch traced here: 108 us
  Pallas kernels  108 us (99%)
    pallas_call x1, Pallas kernels, shards(): pl.pallas_call(kernel, out_shape=(shape((LOCAL_ROWS, LOCAL), f32), shape(...  106 us

profile of v3, /device:TPU:1, one launch (start us, length us, event | category | flops | bytes accessed | tf_op | source)
XLA Modules:
  0.0 108.2 jit_solution(36051639088974975)
XLA Ops:
  0.6 106.1 %shard_map.58 = (f32[128,2304]{1,0:T(8,128)S(1)}, f32[256,2304]{1,0:T(8,128)S(1)}, f32[128,256]{1,0:T(8,128)S(1)}, f32[4,2304]{1,0:T(4,128)S(1)}) custom-call(f32[128,2304]{1,0:T(8,128)} %mom_hbm.1, bf16[128,2304]{1,0:T(8,128)(2,1)} %grad_hbm.1, f32[4,2304]{1,0:T(4,128)} %rf_hbm.1), custom_call_target="tpu_custom_call" | custom-call | tf_op jit(solution)/shard_map/pallas_call | solution.py:525
  106.8 1.5 %shard_map.59 = (f32[128,2304]{1,0:T(8,128)}, bf16[128,2304]{1,0:T(8,128)(2,1)}, f32[4,2304]{1,0:T(4,128)}) custom-call(f32[128,2304]{1,0:T(8,128)S(1)} %get-tuple-element.7.nm, f32[256,2304]{1,0:T(8,128)S(1)} %get-tuple-element.8.rr, f32[128,256]{1,0:T(8,128)S(1)} %get-tuple-element.9.scaled, f32[4,2304]{1,0:T(4,128)S(1)} %get-tuple-element.10.nf), custom_call_target="tpu_custom_call" | custom-call | tf_op jit(solution)/shard_map/pallas_call | solution.py:540

commit v4 on v3

--- a/solution.py
+++ b/solution.py
@@ -432,7 +432,7 @@
     squares = right_rows(c, jnp.zeros((RANK, 128), f32))
     gather.finish()
     squares = right_rows(1 - c, squares)
-    sq[...] = dot(jnp.ones((8, 128), f32), squares, ((1,), (1,)))
+    sq[...] = dot(jnp.ones((8, 128), f32), squares, ((1,), (1,)))[0:1, :]
     earlier = list(started)
     parts = [go(sq, sqr.at[e - 1], at(dz=e)) for e in AROUND]
 
@@ -454,7 +454,7 @@
     for e in range(1, NZ):
         norm = norm + sqr[e - 1]
     inverse_norm = 1.0 / (jnp.sqrt(norm) + norm_eps)
-    scaled = basis * (math.sqrt(ROWS * COLS / RANK) * inverse_norm[0:1, :])
+    scaled = basis * (math.sqrt(ROWS * COLS / RANK) * inverse_norm)
     scaled_ref[...] = scaled
     chip = y * NX + x
     eight = rr[pl.ds(pl.multiple_of(chip * 8, 8), 8), :]
@@ -518,8 +518,8 @@
         (8, REST),
         (2, NY, NX, 8, HALF),
         (RANK, RANK),
-        (8, RANK),
-        (NZ - 1, 8, RANK),
+        (1, RANK),
+        (NZ - 1, 1, RANK),
     ]
     shape = jax.ShapeDtypeStruct
     parts = pl.pallas_call(

time: 109 us -> 109 us (level)
  no operation moved by 1% of the time
where the time goes in v4:
time: 109 us; the launch traced here: 108 us
  Pallas kernels  108 us (99%)
    pallas_call x1, Pallas kernels, shards(): pl.pallas_call(kernel, out_shape=(shape((LOCAL_ROWS, LOCAL), f32), shape(...  106 us

profile of v4, /device:TPU:1, one launch (start us, length us, event | category | flops | bytes accessed | tf_op | source)
XLA Modules:
  0.0 108.4 jit_solution(12128253129801733938)
XLA Ops:
  0.6 106.3 %shard_map.58 = (f32[128,2304]{1,0:T(8,128)S(1)}, f32[256,2304]{1,0:T(8,128)S(1)}, f32[128,256]{1,0:T(8,128)S(1)}, f32[4,2304]{1,0:T(4,128)S(1)}) custom-call(f32[128,2304]{1,0:T(8,128)} %mom_hbm.1, bf16[128,2304]{1,0:T(8,128)(2,1)} %grad_hbm.1, f32[4,2304]{1,0:T(4,128)} %rf_hbm.1), custom_call_target="tpu_custom_call" | custom-call | tf_op jit(solution)/shard_map/pallas_call | solution.py:525
  106.9 1.5 %shard_map.59 = (f32[128,2304]{1,0:T(8,128)}, bf16[128,2304]{1,0:T(8,128)(2,1)}, f32[4,2304]{1,0:T(4,128)}) custom-call(f32[128,2304]{1,0:T(8,128)S(1)} %get-tuple-element.7.nm, f32[256,2304]{1,0:T(8,128)S(1)} %get-tuple-element.8.rr, f32[128,256]{1,0:T(8,128)S(1)} %get-tuple-element.9.scaled, f32[4,2304]{1,0:T(4,128)S(1)} %get-tuple-element.10.nf), custom_call_target="tpu_custom_call" | custom-call | tf_op jit(solution)/shard_map/pallas_call | solution.py:540
